TPU v7x, 32 devices: a whole 2x2x4 slice. The times are simulated.
32 devices in a mesh: row: 4 (over z), col: 8 (over y, x, core).
Axes of the slice: x: 2, y: 2, z: 4, core: 2. Of those that a mesh axis runs over, the one named last changes fastest.
Arguments:
- front: float32 [16384, 16384], P('row', 'col')
- tiles: float32 [4096, 128, 128], P(('row', 'col')), may hold values from -0.375 to 0.375
- tile_block: int32 [2, 4096], replicated, may hold values from 0 to 127, as said below
- valid_rows: int32 [4096], P(('row', 'col')), may hold values from 64 to 128
Outputs:
- factored: float32 [16384, 16384], P('row', 'col')
Inputs may be any that keep to these rules, and one draw needn't show every extreme that they name: tile_block[0, t] and tile_block[1, t] give the block row and block column, in blocks of 128, that tile t is added to. The 128 tiles of each device (tiles laid in order over row+col) go to blocks held by exactly 16 different devices, 8 tiles to each.
All inputs are finite; a program needn't handle non-finite values.
Results may differ from a plain program's by a relative error of at most 0.0001.
Values sent between devices are 32-bit elements; how exact they have to be, the bound alone decides.
No kernel may reach another device: no remote copies, remote signals or barrier semaphores. Data moves between devices by JAX's collectives and lax.ppermute only.
A program may use at most 192 MiB of HBM per device.

v0:
```python
import functools

import jax
import jax.numpy as jnp
from jax import lax
from jax.experimental import pallas as pl
from jax.experimental.pallas import tpu as pltpu
from jax.sharding import PartitionSpec as P

NB = 128
PANELS = 2
TOTAL = NB * PANELS
MIB = 1 << 20
UNIT = 8
PANEL_SLOTS = 32


precise = lax.Precision.HIGHEST


def dot_nt(a, b, precision=precise):
    return lax.dot_general(
        a, b, (((1,), (1,)), ((), ())), precision=precision, preferred_element_type=jnp.float32
    )


def pack_kernel(slot_ref, valid_ref, tiles_ref, out_ref, buf, sem_in, sem_out):
    count, side = tiles_ref.shape[0], tiles_ref.shape[1]

    def fetch(t):
        return pltpu.make_async_copy(tiles_ref.at[t], buf.at[t], sem_in.at[t])

    def store(t):
        return pltpu.make_async_copy(buf.at[t], out_ref.at[jnp.maximum(slot_ref[t], 0)], sem_out.at[t])

    def each(act):
        @pl.loop(0, count)
        def _(t):
            @pl.when(slot_ref[t] >= 0)
            def _():
                act(t)

    def mask(t):
        fetch(t).wait()
        rows = lax.broadcasted_iota(jnp.int32, (side, side), 0)
        buf[t] = jnp.where(rows < valid_ref[t], buf[t], 0.0)
        store(t).start()

    each(lambda t: fetch(t).start())
    each(mask)
    each(lambda t: store(t).wait())


def pack(tiles, slots, valid, n_slots):
    count, side = tiles.shape[0], tiles.shape[1]
    smem = pl.BlockSpec(memory_space=pltpu.SMEM)
    return pl.pallas_call(
        pack_kernel,
        out_shape=jax.ShapeDtypeStruct((n_slots, side, side), jnp.float32),
        in_specs=[smem, smem, pl.BlockSpec(memory_space=pl.ANY)],
        out_specs=pl.BlockSpec(memory_space=pl.ANY),
        scratch_shapes=[
            pltpu.VMEM((count, side, side), jnp.float32),
            pltpu.SemaphoreType.DMA((count,)),
            pltpu.SemaphoreType.DMA((count,)),
        ],
        compiler_params=pltpu.CompilerParams(vmem_limit_bytes=24 * MIB),
    )(slots, valid, tiles)


def spread_kernel(
    width, stride, meta_ref, empty_ref, count_ref, tiles_ref, out_ref, code_ref, stage, sem
):
    count, units = tiles_ref.shape[0], tiles_ref.shape[1]
    devices, length = code_ref.shape

    @pl.loop(0, devices)
    def _(d):
        for k in range(length):
            code_ref[d, k] = -1

    @pl.loop(0, count)
    def _(i):
        tile, target, base = meta_ref[0, i], meta_ref[1, i], meta_ref[2, i]
        filled, code, valid = meta_ref[3, i], meta_ref[4, i], meta_ref[5, i]
        shape = tiles_ref.shape[1:]
        rows = lax.broadcasted_iota(jnp.int32, shape, 0) * shape[1]
        rows += lax.broadcasted_iota(jnp.int32, shape, 1)
        stage[target, pl.ds(base, units)] = jnp.where(rows < valid, tiles_ref[tile], 0.0)
        for u in range(units):
            code_ref[target, base + u] = jnp.where(u < filled, code + u * stride, -1)

    for half in range(2):
        first = 0 if half == 0 else count_ref[0]
        last = count_ref[0] if half == 0 else count
        free = count_ref[1 + half]

        def each_tile(i, carry):
            target, base, filled = meta_ref[1, i], meta_ref[2, i], meta_ref[3, i]

            def each_unit(q, carry):
                at, depth = carry
                relay = empty_ref[half, at]
                place = jnp.minimum(depth, width - 1)
                stage[relay, place] = stage[target, q]
                code_ref[relay, place] = code_ref[target, q]
                wrap = at + 1 >= free
                return jnp.where(wrap, 0, at + 1), jnp.where(wrap, depth + 1, depth)

            return lax.fori_loop(jnp.maximum(base, width), base + filled, each_unit, carry)

        lax.fori_loop(first, last, each_tile, (jnp.int32(0), jnp.int32(0)))

    copy = pltpu.make_async_copy(stage.at[:, pl.ds(0, width)], out_ref, sem)
    copy.start()
    copy.wait()


def spread(tiles, meta, empties, counts, devices, width, length, stride):
    count, side = tiles.shape[0], tiles.shape[1]
    units = side // UNIT
    smem = pl.BlockSpec(memory_space=pltpu.SMEM)
    return pl.pallas_call(
        functools.partial(spread_kernel, width, stride),
        out_shape=[
            jax.ShapeDtypeStruct((devices, width, UNIT, side), jnp.float32),
            jax.ShapeDtypeStruct((devices, length), jnp.int32),
        ],
        in_specs=[smem, smem, smem, pl.BlockSpec(memory_space=pltpu.VMEM)],
        out_specs=[pl.BlockSpec(memory_space=pl.ANY), smem],
        scratch_shapes=[
            pltpu.VMEM((devices, length, UNIT, side), jnp.float32),
            pltpu.SemaphoreType.DMA,
        ],
        compiler_params=pltpu.CompilerParams(vmem_limit_bytes=40 * MIB),
    )(meta, empties, counts, tiles.reshape(count, units, UNIT, side))


def relay_kernel(slot_ref, arrived_ref, out_ref):
    devices, width = slot_ref.shape

    @pl.loop(0, devices)
    def _(s):
        def more(k):
            return (k < width) & (slot_ref[s, jnp.minimum(k, width - 1)] >= 0)

        def move(k):
            out_ref[slot_ref[s, k]] = arrived_ref[s, k]
            return k + 1

        lax.while_loop(more, move, jnp.int32(0))


def relay(slots, arrived, length):
    vmem = pl.BlockSpec(memory_space=pltpu.VMEM)
    return pl.pallas_call(
        relay_kernel,
        out_shape=jax.ShapeDtypeStruct((length,) + arrived.shape[2:], jnp.float32),
        in_specs=[pl.BlockSpec(memory_space=pltpu.SMEM), vmem],
        out_specs=vmem,
        compiler_params=pltpu.CompilerParams(vmem_limit_bytes=40 * MIB),
    )(slots, arrived)


def add_kernel(
    cols_blocks, block_ref, unit_ref, index_ref, count_ref, partial_ref, arrived_ref, out_ref, buf,
    group_start, sem_in, sem_out
):
    slots, side = buf.shape[0], buf.shape[1]
    unit = arrived_ref.shape[1]
    ahead = slots // 2
    count = count_ref[0]

    def listed(i, carry):
        groups, last = carry
        block = block_ref[i]
        fresh = block != last

        @pl.when(fresh)
        def _():
            group_start[groups] = i

        return jnp.where(fresh, groups + 1, groups), block

    groups, _ = lax.fori_loop(0, count, listed, (jnp.int32(0), jnp.int32(-1)))
    group_start[groups] = count

    def window(g):
        block = block_ref[group_start[g]]
        rows = pl.ds(pl.multiple_of(block // cols_blocks * side, side), side)
        columns = pl.ds(pl.multiple_of(block % cols_blocks * side, side), side)
        return out_ref.at[rows, columns]

    def fetch(g):
        at = g % slots
        return pltpu.make_async_copy(window(g), buf.at[at], sem_in.at[at])

    def store(g):
        at = g % slots
        return pltpu.make_async_copy(buf.at[at], window(g), sem_out.at[at])

    @pl.loop(0, jnp.minimum(groups, ahead))
    def _(g):
        fetch(g).start()

    @pl.loop(0, groups)
    def _(g):
        @pl.when(g + ahead < groups)
        def _():
            @pl.when(g >= ahead)
            def _():
                store(g - ahead).wait()

            fetch(g + ahead).start()

        fetch(g).wait()

        @pl.loop(group_start[g], group_start[g + 1])
        def _(i):
            rows = pl.ds(pl.multiple_of(unit_ref[i] * unit, unit), unit)
            buf[g % slots, rows] += arrived_ref[index_ref[i]]

        store(g).start()

    @pl.loop(jnp.maximum(groups - slots, 0), groups)
    def _(g):
        store(g).wait()


def add_relayed(partial, arrived, listing, cols_blocks):
    row_len, col_len = partial.shape
    unit, side = arrived.shape[1:]
    smem = pl.BlockSpec(memory_space=pltpu.SMEM)
    hbm = pl.BlockSpec(memory_space=pl.ANY)
    return pl.pallas_call(
        functools.partial(add_kernel, cols_blocks),
        out_shape=jax.ShapeDtypeStruct((row_len, col_len), jnp.float32),
        in_specs=[smem, smem, smem, smem, hbm, pl.BlockSpec(memory_space=pltpu.VMEM)],
        out_specs=hbm,
        scratch_shapes=[
            pltpu.VMEM((16, side, side), jnp.float32),
            pltpu.SMEM((arrived.shape[0] + 1,), jnp.int32),
            pltpu.SemaphoreType.DMA((16,)),
            pltpu.SemaphoreType.DMA((16,)),
        ],
        input_output_aliases={4: 0},
        compiler_params=pltpu.CompilerParams(vmem_limit_bytes=24 * MIB),
    )(*listing, partial, arrived)


def place_kernel(slot_ref, arrived_ref, out_ref):
    out_ref[...] = jnp.zeros_like(out_ref)

    @pl.loop(0, arrived_ref.shape[0])
    def _(k):
        @pl.when(slot_ref[k] >= 0)
        def _():
            out_ref[slot_ref[k]] = arrived_ref[k]


def place_tiles(arrived, slots, length):
    vmem = pl.BlockSpec(memory_space=pltpu.VMEM)
    return pl.pallas_call(
        place_kernel,
        out_shape=jax.ShapeDtypeStruct((length,) + arrived.shape[1:], jnp.float32),
        in_specs=[pl.BlockSpec(memory_space=pltpu.SMEM), vmem],
        out_specs=vmem,
        compiler_params=pltpu.CompilerParams(vmem_limit_bytes=24 * MIB),
    )(slots, arrived)


def panel_kernel(code_ref, first_ref, front_ref, arrived_ref, out_ref):
    side = arrived_ref.shape[1]

    @pl.when(first_ref[0] == 1)
    def _():
        out_ref[...] = front_ref[...]

    @pl.when(first_ref[0] == 0)
    def _():
        out_ref[...] = jnp.zeros_like(out_ref)

    @pl.loop(0, arrived_ref.shape[0])
    def _(k):
        code = code_ref[k]
        for part in range(PANELS):

            @pl.when((code >= 0) & (code % PANELS == part))
            def _():
                rows = pl.ds(pl.multiple_of(code // PANELS * side, side), side)
                out_ref[rows, part * side : (part + 1) * side] += arrived_ref[k]


def raw_panel(front, arrived, codes, first):
    row_len = front.shape[0]
    smem = pl.BlockSpec(memory_space=pltpu.SMEM)
    return pl.pallas_call(
        panel_kernel,
        grid=(1,),
        out_shape=jax.ShapeDtypeStruct((row_len, TOTAL), jnp.float32),
        in_specs=[
            smem,
            smem,
            pl.BlockSpec((row_len, TOTAL), lambda i: (0, 0)),
            pl.BlockSpec(arrived.shape, lambda i: (0, 0, 0)),
        ],
        out_specs=pl.BlockSpec((row_len, TOTAL), lambda i: (0, 0)),
        compiler_params=pltpu.CompilerParams(vmem_limit_bytes=40 * MIB),
    )(codes, first, front, arrived)


def split(value):
    high = value.astype(jnp.bfloat16)
    low = (value - high.astype(jnp.float32)).astype(jnp.bfloat16)
    return high, low


def rows_kernel(raw_ref, inverse_ref, out_ref, parts_ref):
    solved = dot_nt(raw_ref[...], inverse_ref[...])
    out_ref[...] = solved
    high, low = split(solved)
    parts_ref[:, :TOTAL] = high
    parts_ref[:, TOTAL : 2 * TOTAL] = high
    parts_ref[:, 2 * TOTAL :] = low


def solve_rows(raw, inverse):
    length = raw.shape[0]
    step = min(512, length)
    block = pl.BlockSpec((step, TOTAL), lambda i: (i, 0))
    return pl.pallas_call(
        rows_kernel,
        grid=(length // step,),
        out_shape=[
            jax.ShapeDtypeStruct((length, TOTAL), jnp.float32),
            jax.ShapeDtypeStruct((length, 3 * TOTAL), jnp.bfloat16),
        ],
        in_specs=[block, pl.BlockSpec((TOTAL, TOTAL), lambda i: (0, 0))],
        out_specs=[block, pl.BlockSpec((step, 3 * TOTAL), lambda i: (i, 0))],
        compiler_params=pltpu.CompilerParams(vmem_limit_bytes=24 * MIB),
    )(raw, inverse)


def cols_kernel(raw_ref, inverse_ref, out_ref, parts_ref):
    solved = dot_nt(inverse_ref[...], raw_ref[...])
    out_ref[...] = solved
    high, low = split(solved)
    parts_ref[:TOTAL] = high
    parts_ref[TOTAL : 2 * TOTAL] = low
    parts_ref[2 * TOTAL :] = high


def solve_cols(raw, inverse):
    length = raw.shape[0]
    step = min(512, length)
    block = pl.BlockSpec((TOTAL, step), lambda i: (0, i))
    return pl.pallas_call(
        cols_kernel,
        grid=(length // step,),
        out_shape=[
            jax.ShapeDtypeStruct((TOTAL, length), jnp.float32),
            jax.ShapeDtypeStruct((3 * TOTAL, length), jnp.bfloat16),
        ],
        in_specs=[
            pl.BlockSpec((step, TOTAL), lambda i: (i, 0)),
            pl.BlockSpec((TOTAL, TOTAL), lambda i: (0, 0)),
        ],
        out_specs=[block, pl.BlockSpec((3 * TOTAL, step), lambda i: (0, i))],
        compiler_params=pltpu.CompilerParams(vmem_limit_bytes=24 * MIB),
    )(raw, inverse)


def final_kernel(
    cols_blocks, runs, code_ref, run_ref, place_ref, front_ref, rows_ref, rows_parts, cols_ref, cols_parts,
    lower_ref, arrived_ref, out_ref, cursor
):
    step = pl.program_id(0)
    sources, capacity = code_ref.shape
    height, width = front_ref.shape
    unit, side = arrived_ref.shape[2:]
    per_step = height // unit

    @pl.when(step == 0)
    def _():
        for s in range(sources):
            cursor[s] = 0

    chunk = min(512, width)
    for start in range(0, width, chunk):
        at = slice(start, start + chunk)
        change = jnp.dot(rows_parts[...], cols_parts[:, at], preferred_element_type=jnp.float32)
        out_ref[:, at] = front_ref[:, at] - change

    edge = (step + 1) * per_step * cols_blocks

    @pl.loop(0, sources)
    def _(s):
        def more(k):
            code = code_ref[s, jnp.minimum(k, capacity - 1)]
            return (k < capacity) & (code >= 0) & (code < edge)

        def add(k):
            code = code_ref[s, k]
            length = run_ref[s, k]
            unit_row = code // cols_blocks - step * per_step
            columns = pl.ds(pl.multiple_of(code % cols_blocks * side, side), side)
            for run in runs:
                skipped = length // (2 * run) * (2 * run)

                @pl.when(length // run % 2 == 1)
                def _():
                    rows = pl.ds(pl.multiple_of((unit_row + skipped) * unit, unit), run * unit)
                    block = arrived_ref[s, pl.ds(k + skipped, run)]
                    out_ref[rows, columns] += block.reshape(run * unit, side)

            return k + length

        cursor[s] = lax.while_loop(more, add, cursor[s])

    top = (place_ref[0] == 0) & (step == 0)

    @pl.when(top)
    def _():
        out_ref[...] = cols_ref[...]

    @pl.when(place_ref[1] == 0)
    def _():
        out_ref[:, :TOTAL] = jnp.where(top, lower_ref[...], rows_ref[...])


def finish(front, rows, cols, lower, arrived, codes, lengths, place, cols_blocks):
    row_len, col_len = front.shape
    height = TOTAL
    smem = pl.BlockSpec(memory_space=pltpu.SMEM)
    block = pl.BlockSpec((height, TOTAL), lambda i: (i, 0))
    parts = pl.BlockSpec((height, 3 * TOTAL), lambda i: (i, 0))
    wide = pl.BlockSpec((height, col_len), lambda i: (i, 0))
    whole = pl.BlockSpec((TOTAL, col_len), lambda i: (0, 0))
    whole_parts = pl.BlockSpec((3 * TOTAL, col_len), lambda i: (0, 0))
    runs = (16, 8, 4, 2, 1) if arrived.shape[2] == UNIT else (1,)
    return pl.pallas_call(
        functools.partial(final_kernel, cols_blocks, runs),
        grid=(row_len // height,),
        out_shape=jax.ShapeDtypeStruct((row_len, col_len), jnp.float32),
        in_specs=[
            smem, smem, smem, wide, block, parts, whole, whole_parts,
            pl.BlockSpec((TOTAL, TOTAL), lambda i: (0, 0)),
            pl.BlockSpec(memory_space=pltpu.VMEM),
        ],
        out_specs=wide,
        scratch_shapes=[pltpu.SMEM((codes.shape[0],), jnp.int32)],
        compiler_params=pltpu.CompilerParams(vmem_limit_bytes=56 * MIB),
    )(codes, lengths, place, front, *rows, *cols, lower, arrived)


def factor(diagonal):
    def lower_of(block):
        return jnp.linalg.cholesky(jnp.tril(block) + jnp.tril(block, -1).T)

    def inverse_of(block):
        return jax.scipy.linalg.solve_triangular(block, jnp.eye(NB, dtype=jnp.float32), lower=True)

    first = lower_of(diagonal[:NB, :NB])
    first_inverse = inverse_of(first)
    below = dot_nt(diagonal[NB:, :NB], first_inverse)
    second = lower_of(diagonal[NB:, NB:] - dot_nt(below, below))
    second_inverse = inverse_of(second)
    corner = -jnp.dot(second_inverse, jnp.dot(below, first_inverse, precision=precise), precision=precise)
    zero = jnp.zeros((NB, NB), jnp.float32)
    return jnp.block([[first, zero], [below, second]]), jnp.block([[first_inverse, zero], [corner, second_inverse]])


def body(front, tiles, tile_block, valid_rows):
    row_len, col_len = front.shape
    row_count = lax.axis_size("row")
    col_count = lax.axis_size("col")
    device_count = row_count * col_count
    per_device = tiles.shape[0]
    side = tiles.shape[1]
    capacity = 2 * per_device // device_count
    rows_blocks = row_len // side
    cols_blocks = col_len // side
    row_now = lax.axis_index("row")
    col_now = lax.axis_index("col")
    device_now = row_now * col_count + col_now

    block_row = tile_block[0].reshape(device_count, per_device)
    block_col = tile_block[1].reshape(device_count, per_device)
    target_row = block_row // rows_blocks
    target = target_row * col_count + block_col // cols_blocks
    code = block_row % rows_blocks * cols_blocks + block_col % cols_blocks
    position = lax.broadcasted_iota(jnp.int32, target.shape, 1)
    place = jnp.stack([row_now, col_now]).astype(jnp.int32)

    def own(values):
        return lax.dynamic_index_in_dim(values, device_now, 0, keepdims=False)

    in_panel = block_col < PANELS
    panel_key = jnp.where(in_panel, target_row, -1)
    panel_rank = jnp.sum(
        (panel_key[:, :, None] == panel_key[:, None, :]) & (position[:, None, :] < position[:, :, None]),
        axis=2,
    )
    same_col = lax.dynamic_index_in_dim(
        jnp.stack([panel_key, panel_rank, code]).reshape(3, row_count, col_count, per_device),
        col_now, 2, keepdims=False,
    )

    def send_panel(tiles, valid_rows, depth):
        ahead = (own(target_row) - row_now) % row_count
        fits = own(in_panel) & (own(panel_rank) < depth)
        panel_slot = jnp.where(fits, ahead * depth + own(panel_rank), -1)
        panel_out = pack(tiles, panel_slot, valid_rows, row_count * depth)
        panel_in = [panel_out[:depth]]
        for shift in range(1, row_count):
            sending = panel_out[shift * depth : (shift + 1) * depth]
            turn = [(r, (r + shift) % row_count) for r in range(row_count)]
            panel_in.append(lax.ppermute(sending, "row", turn))
        return panel_in

    def sum_panel(front, panel_in, depth):
        fits = (same_col[0] == row_now)[:, :, None] & (same_col[1][:, :, None] == jnp.arange(depth))
        panel_code = same_col[2] // cols_blocks * PANELS + same_col[2] % cols_blocks
        panel_codes = jnp.sum(jnp.where(fits, panel_code[:, :, None] + 1, 0), axis=1) - 1
        by_shift = (row_now - jnp.arange(row_count)) % row_count
        panel_codes = jnp.take(panel_codes, by_shift, axis=0).reshape(-1)
        first = (col_now == 0).astype(jnp.int32).reshape(1)
        return raw_panel(front, jnp.concatenate(panel_in, 0), panel_codes, first)

    front_panel = lax.psum(jnp.where(col_now == 0, front[:, :TOTAL], 0.0), "col")

    panel_depth = (capacity * 5 + 7) // 8
    panel_in = send_panel(tiles, valid_rows, panel_depth)
    for_row = in_panel & (target_row == row_now)
    row_tiles = jnp.sum(for_row, axis=1)
    sources = jnp.arange(device_count)
    row_offset = jnp.sum(
        jnp.where(sources[None, :] < sources[:, None], row_tiles[None, :], 0), axis=1
    )
    row_slot = jnp.where(for_row, row_offset[:, None] + panel_rank, -1).reshape(-1)
    at_slot = row_slot[None, :] == jnp.arange(PANEL_SLOTS)[:, None]
    row_code = (code // cols_blocks * PANELS + code % cols_blocks).reshape(-1)
    row_codes = jnp.sum(jnp.where(at_slot, row_code + 1, 0), axis=1) - 1
    by_shift = (row_now - jnp.arange(row_count)) % row_count * col_count + col_now
    depths = jnp.arange(panel_depth)
    slot_in = jnp.take(row_offset, by_shift)[:, None] + depths
    slot_in = jnp.where(depths < jnp.take(row_tiles, by_shift)[:, None], slot_in, -1)
    slot_in = jnp.where(slot_in < PANEL_SLOTS, slot_in, -1).reshape(-1)
    panel_tiles = place_tiles(jnp.concatenate(panel_in, 0), slot_in, PANEL_SLOTS)

    units = side // UNIT
    length = capacity * units
    width = length * 41 // 64
    pass_on = length * 13 // 32
    half_count = device_count // 2
    half_base = device_now // half_count * half_count
    unit_rows = rows_blocks * units
    local_codes = unit_rows * cols_blocks
    own_target, own_code = own(target), own(code)
    own_position = own(position)
    filled = (valid_rows + UNIT - 1) // UNIT
    key = (own_target * rows_blocks * cols_blocks + own_code) * per_device + own_position
    before = key[None, :] < key[:, None]
    together = own_target[None, :] == own_target[:, None]
    base = jnp.sum(jnp.where(before & together, filled[None, :], 0), axis=1)
    order = jnp.sum(before, axis=1)
    unit_code = (own_target * unit_rows + own_code // cols_blocks * units) * cols_blocks
    unit_code += own_code % cols_blocks
    meta = jnp.stack([own_position, own_target, base, filled, unit_code, valid_rows])
    meta = jnp.sum(
        jnp.where(order[None, :, None] == jnp.arange(per_device), meta[:, :, None], 0), axis=1
    )
    to_device = own_target[:, None] == jnp.arange(device_count)
    load = jnp.sum(jnp.where(to_device, filled[:, None], 0), axis=0).reshape(2, half_count)
    empty = load == 0
    empty_rank = jnp.cumsum(empty, axis=1) - 1
    device_ids = jnp.arange(device_count).reshape(2, half_count)
    listed = (empty[:, :, None]) & (empty_rank[:, :, None] == jnp.arange(half_count))
    empties = jnp.sum(jnp.where(listed, device_ids[:, :, None], 0), axis=1)
    free = jnp.sum(empty, axis=1)
    left = jnp.sum(jnp.maximum(load - width, 0), axis=1)
    failed = jnp.any(left > free * width) | (jnp.sum(row_tiles) > PANEL_SLOTS)
    failed |= jnp.any(own(in_panel) & (own(panel_rank) >= panel_depth))
    counts = jnp.concatenate([jnp.sum(own_target < half_count)[None], free]).astype(jnp.int32)
    outgoing, sent_codes = spread(
        tiles, meta.astype(jnp.int32), empties.astype(jnp.int32), counts,
        device_count, width, length, cols_blocks,
    )

    panel_tiles, sent_codes = lax.optimization_barrier((panel_tiles, sent_codes))
    got = lax.all_to_all(sent_codes[:, :width], ("row", "col"), 0, 0, tiled=True)
    got_target = got // local_codes
    local = got % local_codes
    mine = (got >= 0) & (got_target == device_now)
    direct_codes = jnp.where(mine, local, -1)
    steps = jnp.arange(width)
    opening = (local // cols_blocks % units == 0) | jnp.logical_not(mine)
    later = (steps[None, :] > steps[:, None]) & opening[:, None, :]
    direct_runs = jnp.min(jnp.where(later, steps, width), axis=2) - steps
    total_units = device_count * width
    passing = ((got >= 0) & (got_target != device_now)).reshape(-1)
    flat_key = jnp.where(passing, got.reshape(-1) * total_units + jnp.arange(total_units), -1)
    flat_target = jnp.where(passing, got_target.reshape(-1), -1)
    rank = jnp.sum(
        (flat_target[None, :] == flat_target[:, None]) & (flat_key[None, :] < flat_key[:, None]), axis=1
    )
    failed = failed | jnp.any(passing & (rank >= pass_on))
    relay_slot = jnp.where(
        passing & (rank < pass_on), (flat_target - half_base) * pass_on + rank, -1
    )
    picked = relay_slot[:, None] == jnp.arange(half_count * pass_on)
    relay_codes = jnp.sum(jnp.where(picked, local.reshape(-1)[:, None] + 1, 0), axis=0) - 1
    notes = jnp.zeros((2, half_count, pass_on + 1), jnp.int32)
    notes = lax.dynamic_update_slice(
        notes, relay_codes.reshape(1, half_count, pass_on).astype(jnp.int32), (device_now // half_count, 0, 0)
    )
    notes = notes.at[:, :, pass_on].set(failed.astype(jnp.int32))
    notes = lax.all_to_all(
        notes.reshape(device_count, pass_on + 1), ("row", "col"), 0, 0, tiled=True
    )
    too_full = jnp.any(notes[:, pass_on] != 0)
    relay_codes = lax.dynamic_slice_in_dim(notes, half_base, half_count, 0)[:, :pass_on]
    relay_slot = relay_slot.reshape(device_count, width)

    flat = relay_codes.reshape(-1)
    unit_row, relay_col = flat // cols_blocks, flat % cols_blocks
    wanted = (flat >= 0) & ((row_now > 0) | (unit_row >= TOTAL // UNIT))
    wanted &= (col_now > 0) | (relay_col >= PANELS)
    relay_block = unit_row // units * cols_blocks + relay_col
    relay_key = jnp.where(wanted, relay_block * units + unit_row % units, local_codes)
    relay_key = relay_key * flat.shape[0] + jnp.arange(flat.shape[0])
    relay_order = jnp.sum(relay_key[None, :] < relay_key[:, None], axis=1)
    listing = jnp.stack([relay_block, unit_row % units, jnp.arange(flat.shape[0])])
    at_order = relay_order[None, :, None] == jnp.arange(flat.shape[0])
    listing = jnp.sum(jnp.where(at_order, listing[:, :, None], 0), axis=1).astype(jnp.int32)
    listing = [*listing, jnp.sum(wanted).astype(jnp.int32).reshape(1)]

    outgoing, notes, front_panel, panel_tiles = lax.optimization_barrier(
        (outgoing, notes, front_panel, panel_tiles)
    )
    panel_tiles = lax.psum(panel_tiles, "col")
    raw_rows = raw_panel(front_panel, panel_tiles, row_codes, jnp.ones((1,), jnp.int32))
    arrived = lax.all_to_all(outgoing, ("row", "col"), 0, 0, tiled=True)
    slice_start = col_now * col_len % row_len
    slice_root = col_now * col_len // row_len

    def chain(raw_rows):
        picked = lax.dynamic_slice_in_dim(raw_rows, slice_start, col_len, 0)
        raw_cols = lax.psum(jnp.where(row_now == slice_root, picked, 0.0), "row")
        diagonal = jnp.where(row_now == 0, raw_rows[:TOTAL], jnp.eye(TOTAL, dtype=jnp.float32))
        lower, inverse = factor(diagonal)
        inverse, raw_cols = lax.optimization_barrier((inverse, raw_cols))
        inverse = lax.psum(jnp.where(row_now == 0, inverse, 0.0), "row")
        return solve_rows(raw_rows, inverse), solve_cols(raw_cols, inverse), lower

    rows, cols, lower = chain(raw_rows)
    tables = (relay_slot, direct_codes, direct_runs, listing)
    arrived, rows, cols, lower, tables = lax.optimization_barrier((arrived, rows, cols, lower, tables))
    relay_slot, direct_codes, direct_runs, listing = tables

    def relayed(front, tiles, valid_rows, arrived, rows, cols, lower):
        passed = relay(relay_slot, arrived, half_count * pass_on)
        halves = [list(range(half_count)), list(range(half_count, device_count))]
        passed = lax.all_to_all(
            passed.reshape(half_count, pass_on, UNIT, side), ("row", "col"), 0, 0,
            axis_index_groups=halves, tiled=True,
        )
        partial = finish(
            front, rows, cols, lower, arrived, direct_codes, direct_runs, place, cols_blocks
        )
        return add_relayed(partial, passed.reshape(-1, UNIT, side), listing, cols_blocks)

    def padded(front, tiles, valid_rows, arrived, rows, cols, lower):
        partial = sum_panel(front, send_panel(tiles, valid_rows, capacity), capacity)
        raw_rows = lax.psum(partial, "col")
        order = (target * rows_blocks * cols_blocks + code) * per_device + position
        ranking = jnp.sum(
            (target[:, :, None] == target[:, None, :]) & (order[:, None, :] < order[:, :, None]), axis=2
        )
        slot = own(target) * capacity + own(ranking)
        here = (target == device_now)[:, :, None] & (ranking[:, :, None] == jnp.arange(capacity))
        codes = jnp.sum(jnp.where(here, code[:, :, None] + 1, 0), axis=1) - 1
        packed = pack(tiles, slot, valid_rows, device_count * capacity)
        arrived = lax.all_to_all(
            packed.reshape(device_count, capacity, side, side), ("row", "col"), 0, 0, tiled=True
        )
        rows, cols, lower = chain(raw_rows)
        return finish(
            front, rows, cols, lower, arrived, codes, jnp.ones_like(codes), place, cols_blocks
        )

    return lax.cond(
        too_full, padded, relayed, front, tiles, valid_rows, arrived, rows, cols, lower
    )


def solution(mesh):
    placed = (P("row", "col"), P(("row", "col"), None, None), P(), P(("row", "col")))
    return jax.shard_map(
        body, mesh=mesh, in_specs=placed, out_specs=P("row", "col"), check_vma=False
    )
```

profile of v0, /device:TPU:7, one launch (start us, length us, event | category | flops | bytes accessed | tf_op | source)
XLA Modules:
  0.0 559.9 jit_solution(8532729030863659315)
XLA Ops:
  9.4 7.1 %shard_map.48 = f32[20,128,128]{2,1,0:T(8,128)S(1)} custom-call(s32[128]{0:T(128)S(1)} %get-tuple-element.317.slot_ref, s32[128]{0:T(128)} %valid_ref.1, f32[128,128,128]{2,1,0:T(8,128)} %tiles_ref.1), custom_call_target="tpu_custom_call" | custom-call | tf_op jit(solution)/shard_map/pallas_call | solution.py:57
  16.6 3.3 collective-permute-start.5
  20.4 4.4 slice_select_fusion.1
  29.6 21.1 %shard_map.50 = (f32[32,82,8,128]{3,2,1,0:T(8,128)S(1)}, s32[32,128]{1,0:T(8,128)}) custom-call(s32[6,128]{1,0:T(8,128)S(1)} %select_reduce_fusion.8.meta_ref, s32[2,16]{1,0:T(2,128)S(1)} %select_reduce_fusion.12.empty_ref, s32[3]{0:T(128)S(1)} %pad_add_fusion.2.count_ref, f32[128,16,8,128]{3,2,1,0:T(8,128)} %bitcast.155), custom_call_target="tpu_custom_call" | custom-call | tf_op jit(solution)/shard_map/pallas_call | solution.py:123
  50.7 4.2 copy-done.4
  55.7 2.4 shard_map.49
  58.1 6.0 %all-to-all-start.2 = ((s32[32,1,82]{2,1,0:T(1,128)}), s32[32,1,82]{2,1,0:T(1,128)S(1)}, u32[]{:S(2)}, u32[]{:S(2)}) async-start(s32[32,1,82]{2,1,0:T(1,128)} %bitcast.35), calls=%async_computation.2 | async-start | bytes 32768 | tf_op jit(solution)/shard_map/all_to_all | solution.py:591
  70.1 6.1 %convert_reduce_fusion.1 = s32[2624]{0:T(1024)S(1)} fusion(s32[2624]{0:T(1024)S(1)} %get-tuple-element.312, s32[2624]{0:T(1024)S(1)} %get-tuple-element.311), kind=kLoop, calls=%fused_computation.104 | loop fusion | flops 34424256 | bytes 31488 | tf_op jit(solution)/shard_map/reduce_sum | solution.py:604
  79.3 8.8 %all_to_all.40 = s32[32,1,53]{2,1,0:T(1,128)S(1)} all-to-all(s32[32,1,53]{2,1,0:T(1,128)S(1)} %bitcast.169), channel_id=1, replica_groups=mesh['row'=4,'col'=8] {'row','col'}, dimensions={0} | all-to-all | bytes 13568 | tf_op jit(solution)/shard_map/all_to_all | solution.py:618
  88.1 18.3 %all-reduce.18.cloned.1.call-done.front_ref = f32[4096,256]{1,0:T(8,128)} async-done(((f32[4096,256]{1,0:T(8,128)}), f32[4096,256]{1,0:T(8,128)}) %all-reduce.18.cloned.1.call-update) | async-done | bytes 4194320 | tf_op jit(solution)/shard_map/psum | solution.py:530
  106.4 6.1 %all-to-all-start.4 = ((f32[32,82,8,128]{3,2,1,0:T(8,128)}), f32[32,82,8,128]{3,2,1,0:T(8,128)}, u32[]{:S(2)}, u32[]{:S(2)}) async-start(f32[32,82,8,128]{3,2,1,0:T(8,128)} %copy-done.4), calls=%async_computation.4 | async-start | bytes 21495808 | tf_op jit(solution)/shard_map/all_to_all | solution.py:643
  119.6 153.5 %all-reduce.20.cloned.1.call-done.arrived_ref = f32[32,128,128]{2,1,0:T(8,128)} async-done(((f32[32,128,128]{2,1,0:T(8,128)}), f32[32,128,128]{2,1,0:T(8,128)}) %all-reduce.20.cloned.1.call-update) | async-done | bytes 2097168 | tf_op jit(solution)/shard_map/psum | solution.py:641
  273.0 2.2 copy-done.7
  275.2 1.6 copy-done.12
  276.8 1.9 shard_map.51.raw_ref
  278.7 1.9 copy-done.1
  281.0 11.7 %cholesky.96 = f32[128,128]{1,0:T(8,128)S(1)} custom-call(f32[128,128]{1,0:T(8,128)S(1)} %copy.160), custom_call_target="Cholesky" | custom-call | tf_op jit(solution)/shard_map/jit(cholesky)/cholesky | solution.py:458
  294.1 9.8 %custom-call.10 = f32[1,128,128]{1,2,0:T(8,128)S(1)} custom-call(f32[1,128,128]{2,1,0:T(8,128)S(1)} %get-tuple-element.278), custom_call_target="InvertDiagBlocksLowerTriangular" | custom-call | tf_op jit(solution)/shard_map/jit(_solve_triangular)/triangular_solve | solution.py:461
  303.9 3.1 dynamic-slice_select_fusion.1
  308.3 11.7 %cholesky.107 = f32[128,128]{1,0:T(8,128)S(1)} custom-call(f32[128,128]{1,0:T(8,128)S(1)} %fusion.47), custom_call_target="Cholesky" | custom-call | tf_op jit(solution)/shard_map/jit(cholesky)/cholesky | solution.py:458
  321.4 9.8 %custom-call.11 = f32[1,128,128]{1,2,0:T(8,128)S(1)} custom-call(f32[1,128,128]{2,1,0:T(8,128)S(1)} %get-tuple-element.276), custom_call_target="InvertDiagBlocksLowerTriangular" | custom-call | tf_op jit(solution)/shard_map/jit(_solve_triangular)/triangular_solve | solution.py:461
  332.2 82.3 %all-reduce.22.cloned.1.call-done.raw_ref = f32[2048,256]{1,0:T(8,128)} async-done(((f32[2048,256]{1,0:T(8,128)}), f32[2048,256]{1,0:T(8,128)}) %all-reduce.22.cloned.1.call-update) | async-done | bytes 2097168 | tf_op jit(solution)/shard_map/psum | solution.py:649
  418.0 38.3 %all-reduce.24.cloned.1.call-done.inverse_ref = f32[256,256]{1,0:T(8,128)} async-done(((f32[256,256]{1,0:T(8,128)}), f32[256,256]{1,0:T(8,128)}) %all-reduce.24.cloned.1.call-update) | async-done | bytes 262160 | tf_op jit(solution)/shard_map/psum | solution.py:653
  456.3 2.2 copy-done.2
  459.4 7.5 %shard_map.52 = (f32[4096,256]{1,0:T(8,128)}, bf16[4096,768]{1,0:T(8,128)(2,1)}) custom-call(f32[4096,256]{1,0:T(8,128)S(1)} %copy-done.2, f32[256,256]{1,0:T(8,128)S(1)} %copy-done.14), custom_call_target="tpu_custom_call" | custom-call | tf_op jit(solution)/shard_map/pallas_call | solution.py:331
  467.0 4.3 shard_map.53
  471.3 81.6 %conditional.1 = (f32[4096,2048]{1,0:T(8,128)}) conditional(s32[]{:T(128)} %convert_element_type.74, (s32[32,82]{1,0:T(8,128)}, s32[32,82]{0,1:T(8,128)S(1)}, s32[2]{0:T(128)}, f32[4096,2048]{1,0:T(8,128)}, f32[4096,256]{1,0:T(8,128)}, /*index=5*/bf16[4096,768]{1,0:T(8,128)(2,1)}, f32[256,2048]{1,0:T(8,128)}, bf16[768,2048]{1,0:T(8,128)(2,1)}, ...), branch_computations={%region_30.34_spmd, %region_31.41_spmd} | conditional | flops 158879152 | bytes 287434368 | solution.py:692
  471.3 10.0 %branch_0_fun.4 = f32[832,8,128]{2,1,0:T(8,128)} custom-call(s32[32,82]{1,0:T(8,128)S(1)} %get-tuple-element.110.slot_ref, f32[32,82,8,128]{3,2,1,0:T(8,128)} %get-tuple-element.109.arrived_ref), custom_call_target="tpu_custom_call" | custom-call | tf_op jit(solution)/shard_map/cond/branch_0_fun/pallas_call | solution.py:156
  481.2 8.5 %all-to-all-start = ((f32[16,52,8,128]{3,2,1,0:T(8,128)}), f32[16,52,8,128]{3,2,1,0:T(8,128)S(1)}, u32[]{:S(2)}, u32[]{:S(2)}) async-start(f32[16,52,8,128]{3,2,1,0:T(8,128)} %bitcast), calls=%async_computation | async-start | bytes 6815744 | tf_op jit(solution)/shard_map/cond/branch_0_fun/all_to_all | solution.py:664
  490.4 49.4 %branch_0_fun.3.partial_ref = f32[4096,2048]{1,0:T(8,128)} custom-call(s32[32,82]{1,0:T(8,128)S(1)} %copy-done.18, s32[32,82]{1,0:T(8,128)} %copy.169.run_ref, s32[2]{0:T(128)S(1)} %copy-done.24, f32[4096,2048]{1,0:T(8,128)} %get-tuple-element.103.front_ref, f32[4096,256]{1,0:T(8,128)} %get-tuple-element.104.rows_ref, ...), custom_call_target="tpu_custom_call" | custom-call | tf_op jit(solution)/shard_map/cond/branch_0_fun/pallas_call | solution.py:441
  539.8 1.5 all-to-all-done
  541.4 10.4 %branch_0_fun.5 = f32[4096,2048]{1,0:T(8,128)} custom-call(s32[832]{0:T(1024)S(1)} %copy-done.21, s32[832]{0:T(1024)S(1)} %copy-done.20, s32[832]{0:T(1024)S(1)} %copy-done.19, s32[1]{0:T(128)} %get-tuple-element.99.count_ref, f32[4096,2048]{1,0:T(8,128)} %branch_0_fun.3.partial_ref, f32[832,8,128]{2,1,0:T(8,128)S(1)} %bitcast.154), custom_call_target="tpu_custom_call", output_to_operand_aliasing={{}: (4, {})} | custom-call | tf_op jit(solution)/shard_map/cond/branch_0_fun/pallas_call | solution.py:235
  (159 shorter events, 32.1 us)
Async XLA Ops:
  6.5 99.8 %all-reduce.18.cloned.1.call-start = ((), (), s32[]{:S(2)}) async-start(), calls=%async_computation.8 | async-start | bytes 8388608 | tf_op jit(solution)/shard_map/psum | solution.py:530
  7.4 18.4 %copy-start.17 = (s32[32,128]{1,0:T(8,128)}, s32[32,128]{1,0:T(8,128)S(1)}, u32[]{:S(2)}) copy-start(s32[32,128]{1,0:T(8,128)S(1)} %get-tuple-element.300) | copy-start | bytes 49156
  16.6 39.0 %collective-permute-start.5 = (f32[5,128,128]{2,1,0:T(8,128)S(1)}, f32[5,128,128]{2,1,0:T(8,128)S(1)}, u32[]{:S(2)}, u32[]{:S(2)}) collective-permute-start(f32[5,128,128]{2,1,0:T(8,128)S(1)} %get-tuple-element.295), channel_id=1, source_target_pairs={{0,24},{8,0},{16,8},{24,16},{1,25},{9,1},{17,9},{25,17},{2,26},{10... | collective-permute-start | bytes 983048 | tf_op jit(solution)/shard_map/ppermute | solution.py:518
  19.9 35.7 %collective-permute-start.4 = (f32[5,128,128]{2,1,0:T(8,128)S(1)}, f32[5,128,128]{2,1,0:T(8,128)S(1)}, u32[]{:S(2)}, u32[]{:S(2)}) collective-permute-start(f32[5,128,128]{2,1,0:T(8,128)S(1)} %get-tuple-element.296), channel_id=1, source_target_pairs={{0,16},{8,24},{16,0},{24,8},{1,17},{9,25},{17,1},{25,9},{2,18},{10... | collective-permute-start | bytes 983048 | tf_op jit(solution)/shard_map/ppermute | solution.py:518
  19.9 35.7 %collective-permute-start.3 = (f32[5,128,128]{2,1,0:T(8,128)S(1)}, f32[5,128,128]{2,1,0:T(8,128)S(1)}, u32[]{:S(2)}, u32[]{:S(2)}) collective-permute-start(f32[5,128,128]{2,1,0:T(8,128)S(1)} %get-tuple-element.297), channel_id=1, source_target_pairs={{0,8},{8,16},{16,24},{24,0},{1,9},{9,17},{17,25},{25,1},{2,10},{10... | collective-permute-start | bytes 983048 | tf_op jit(solution)/shard_map/ppermute | solution.py:518
  24.9 0.7 copy-start.22
  24.9 3.6 copy-start.16
  50.7 4.2 copy-start.4
  58.1 10.8 %all-to-all-start.2 = ((s32[32,1,82]{2,1,0:T(1,128)}), s32[32,1,82]{2,1,0:T(1,128)S(1)}, u32[]{:S(2)}, u32[]{:S(2)}) async-start(s32[32,1,82]{2,1,0:T(1,128)} %bitcast.35), calls=%async_computation.2 | async-start | bytes 32768 | tf_op jit(solution)/shard_map/all_to_all | solution.py:591
  106.4 364.9 %all-to-all-start.4 = ((f32[32,82,8,128]{3,2,1,0:T(8,128)}), f32[32,82,8,128]{3,2,1,0:T(8,128)}, u32[]{:S(2)}, u32[]{:S(2)}) async-start(f32[32,82,8,128]{3,2,1,0:T(8,128)} %copy-done.4), calls=%async_computation.4 | async-start | bytes 21495808 | tf_op jit(solution)/shard_map/all_to_all | solution.py:643
  112.5 160.6 %all-reduce.20.cloned.1.call-start = ((), (), s32[]{:S(2)}) async-start(), calls=%async_computation.9 | async-start | bytes 4194304 | tf_op jit(solution)/shard_map/psum | solution.py:641
  117.5 297.0 %all-reduce.22.cloned.1.call-start = ((), (), s32[]{:S(2)}) async-start(), calls=%async_computation.10 | async-start | bytes 4194304 | tf_op jit(solution)/shard_map/psum | solution.py:649
  273.0 2.2 copy-start.7
  275.2 1.6 copy-start.12
  278.7 1.9 copy-start.1
  307.0 149.3 %all-reduce.24.cloned.1.call-start = ((), (), s32[]{:S(2)}) async-start(), calls=%async_computation.11 | async-start | bytes 524288 | tf_op jit(solution)/shard_map/psum | solution.py:653
  456.3 2.2 copy-start.2
  458.5 0.9 copy-start.14
  459.4 7.5 %copy-start.10 = (f32[2048,256]{1,0:T(8,128)S(1)}, f32[2048,256]{1,0:T(8,128)}, u32[]{:S(2)}) copy-start(f32[2048,256]{1,0:T(8,128)} %all-reduce.22.cloned.1.call-done.raw_ref) | copy-start | bytes 6291460
  481.2 9.1 %copy-start.18 = (s32[32,82]{1,0:T(8,128)S(1)}, s32[32,82]{1,0:T(8,128)}, u32[]{:S(2)}) copy-start(s32[32,82]{1,0:T(8,128)} %get-tuple-element.100.code_ref) | copy-start | bytes 31492 | tf_op jit(solution)/shard_map/cond
  481.2 9.1 %copy-start.24 = (s32[2]{0:T(128)S(1)}, s32[2]{0:T(128)}, u32[]{:S(2)}) copy-start(s32[2]{0:T(128)} %get-tuple-element.102.place_ref) | copy-start | bytes 28 | tf_op jit(solution)/shard_map/cond
  481.2 60.1 %all-to-all-start = ((f32[16,52,8,128]{3,2,1,0:T(8,128)}), f32[16,52,8,128]{3,2,1,0:T(8,128)S(1)}, u32[]{:S(2)}, u32[]{:S(2)}) async-start(f32[16,52,8,128]{3,2,1,0:T(8,128)} %bitcast), calls=%async_computation | async-start | bytes 6815744 | tf_op jit(solution)/shard_map/cond/branch_0_fun/all_to_all | solution.py:664
  490.4 51.0 %copy-start.19 = (s32[832]{0:T(1024)S(1)}, s32[832]{0:T(1024)}, u32[]{:S(2)}) copy-start(s32[832]{0:T(1024)} %get-tuple-element.98.index_ref) | copy-start | bytes 9988 | tf_op jit(solution)/shard_map/cond
  490.4 51.0 %copy-start.20 = (s32[832]{0:T(1024)S(1)}, s32[832]{0:T(1024)}, u32[]{:S(2)}) copy-start(s32[832]{0:T(1024)} %get-tuple-element.97.unit_ref) | copy-start | bytes 9988 | tf_op jit(solution)/shard_map/cond
  490.4 51.0 %copy-start.21 = (s32[832]{0:T(1024)S(1)}, s32[832]{0:T(1024)}, u32[]{:S(2)}) copy-start(s32[832]{0:T(1024)} %get-tuple-element.96.block_ref) | copy-start | bytes 9988 | tf_op jit(solution)/shard_map/cond
Sparse Core Ops, SparseCore 0:
  25.0 81.2 all-reduce.17
  117.6 155.3 all-reduce.19
  307.1 107.3 all-reduce.21
  416.7 39.5 all-reduce.23
where the time goes:
time: 571 us; the launch traced here: 560 us
  waiting for transfers between devices  295 us (52%)
  Pallas kernels  114 us (20%)
  other arithmetic  76.1 us (13%)
  starting transfers between devices  24.8 us (4%)
  local copies, waits for them, and re-layouts  20.4 us (4%)
  between operations  17.5 us (3%)
  blocking collectives  8.85 us (2%)
    psum x1, waiting for transfers between devices, body(): panel_tiles = lax.psum(panel_tiles, 'col')  153 us
    psum x1, waiting for transfers between devices, chain(): raw_cols = lax.psum(jnp.where(row_now == slice_root, picked, 0.0), 'row')  82.3 us
    pallas_call x1, Pallas kernels, finish(): pl.pallas_call(functools.partial(final_kernel, cols_blocks, runs), grid=(...  49.4 us
    psum x1, waiting for transfers between devices, chain(): inverse = lax.psum(jnp.where(row_now == 0, inverse, 0.0), 'row')  38.3 us
    another operation x6, other arithmetic, lower_of(): return jnp.linalg.cholesky(jnp.tril(block) + jnp.tril(block, -1).T)  24.8 us
    pallas_call x1, Pallas kernels, spread(): pl.pallas_call(functools.partial(spread_kernel, width, stride), out_shape...  21.1 us
    another operation x5, other arithmetic, inverse_of(): jax.scipy.linalg.solve_triangular(block, jnp.eye(NB, dtype=jnp.float32),...  20.9 us
    psum x1, waiting for transfers between devices, body(): lax.psum(jnp.where(col_now == 0, front[:, :TOTAL], 0.0), 'col')  18.3 us
  transfers between devices with their start and end apart: 10, of which 6 were waited for; matrix products, arithmetic and copies ran while one was open for 15% of the time, Pallas kernels for 15%

commit v1 on v0

--- a/solution.py
+++ b/solution.py
@@ -468,6 +468,27 @@
     corner = -jnp.dot(second_inverse, jnp.dot(below, first_inverse, precision=precise), precision=precise)
     zero = jnp.zeros((NB, NB), jnp.float32)
     return jnp.block([[first, zero], [below, second]]), jnp.block([[first_inverse, zero], [corner, second_inverse]])
+
+
+def first_steps(value, col_now):
+    half = value.shape[0] // 2
+    upper, lower = value[:half], value[half:]
+    upper_x = lax.ppermute(upper, "col", [(0, 2)])
+    lower_y = lax.ppermute(lower, "col", [(0, 4)])
+    return upper, lower, upper_x, lower_y
+
+
+def last_steps(upper, lower, upper_x, lower_y, col_now):
+    upper = jnp.where(col_now == 0, upper, upper_x)
+    lower = jnp.where(col_now == 0, lower, lower_y)
+    upper_y = lax.ppermute(upper, "col", [(0, 4), (2, 6)])
+    lower_x = lax.ppermute(lower, "col", [(0, 2), (4, 6)])
+    upper = jnp.where(col_now < 4, upper, upper_y)
+    lower = jnp.where((col_now == 0) | (col_now == 4), lower, lower_x)
+    upper_core = lax.ppermute(upper, "col", [(0, 1), (2, 3), (4, 5), (6, 7)])
+    lower_core = lax.ppermute(lower, "col", [(0, 1), (2, 3), (4, 5), (6, 7)])
+    whole = jnp.concatenate([upper, lower], 0)
+    return jnp.where(col_now % 2 == 0, whole, jnp.concatenate([upper_core, lower_core], 0))
 
 
 def body(front, tiles, tile_block, valid_rows):
@@ -527,7 +548,11 @@
         first = (col_now == 0).astype(jnp.int32).reshape(1)
         return raw_panel(front, jnp.concatenate(panel_in, 0), panel_codes, first)
 
-    front_panel = lax.psum(jnp.where(col_now == 0, front[:, :TOTAL], 0.0), "col")
+    eight = col_count == 8
+    if eight:
+        front_parts = first_steps(front[:, :TOTAL], col_now)
+    else:
+        front_panel = lax.psum(jnp.where(col_now == 0, front[:, :TOTAL], 0.0), "col")
 
     panel_depth = (capacity * 5 + 7) // 8
     panel_in = send_panel(tiles, valid_rows, panel_depth)
@@ -587,7 +612,11 @@
         device_count, width, length, cols_blocks,
     )
 
+    if eight:
+        front_parts, sent_codes = lax.optimization_barrier((front_parts, sent_codes))
+        front_panel = last_steps(*front_parts, col_now)
     panel_tiles, sent_codes = lax.optimization_barrier((panel_tiles, sent_codes))
+    panel_tiles = lax.psum(panel_tiles, "col")
     got = lax.all_to_all(sent_codes[:, :width], ("row", "col"), 0, 0, tiled=True)
     got_target = got // local_codes
     local = got % local_codes
@@ -615,6 +644,7 @@
         notes, relay_codes.reshape(1, half_count, pass_on).astype(jnp.int32), (device_now // half_count, 0, 0)
     )
     notes = notes.at[:, :, pass_on].set(failed.astype(jnp.int32))
+    notes, panel_tiles = lax.optimization_barrier((notes, panel_tiles))
     notes = lax.all_to_all(
         notes.reshape(device_count, pass_on + 1), ("row", "col"), 0, 0, tiled=True
     )
@@ -638,7 +668,6 @@
     outgoing, notes, front_panel, panel_tiles = lax.optimization_barrier(
         (outgoing, notes, front_panel, panel_tiles)
     )
-    panel_tiles = lax.psum(panel_tiles, "col")
     raw_rows = raw_panel(front_panel, panel_tiles, row_codes, jnp.ones((1,), jnp.int32))
     arrived = lax.all_to_all(outgoing, ("row", "col"), 0, 0, tiled=True)
     slice_start = col_now * col_len % row_len

time: 571 us -> 571 us (level)
  waiting for transfers between devices: 295 us -> 269 us
  starting transfers between devices: 24.8 us -> 43 us
  other arithmetic: 76.1 us -> 89.8 us
  blocking collectives: 8.85 us -> 0 us
    psum x1, waiting for transfers between devices: 153 us -> 31.2 us  [body(): panel_tiles = lax.psum(panel_tiles, 'col')]
    psum x1, waiting for transfers between devices: 82.3 us -> 163 us  [chain(): raw_cols = lax.psum(jnp.where(row_now == slice_root, picked, 0.0), 'row')]
    psum x1 -> x0, waiting for transfers between devices: 18.3 us -> none  [body(): lax.psum(jnp.where(col_now == 0, front[:, :TOTAL], 0.0), 'col')]
    all_to_all x1, waiting for transfers between devices: 0.01 us -> 13.3 us  [body(): arrived = lax.all_to_all(outgoing, ('row', 'col'), 0, 0, tiled=True)]
    psum x1, waiting for transfers between devices: 38.3 us -> 51.4 us  [chain(): inverse = lax.psum(jnp.where(row_now == 0, inverse, 0.0), 'row')]
    select_n x1 -> x5, other arithmetic: 4.44 us -> 17 us  [the longest x1 5.33 us: last_steps(): jnp.where(col_now % 2 == 0, whole, jnp.concatenate([upper_core, lower_cor...]
    ppermute x0 -> x6, starting transfers between devices: none -> 10.7 us  [the longest x1 2.08 us: last_steps(): lower_x = lax.ppermute(lower, 'col', [(0, 2), (4, 6)])]
    all_to_all x1 -> x0, blocking collectives: 8.85 us -> none  [body(): lax.all_to_all(notes.reshape(device_count, pass_on + 1), ('row', 'col'),...]
  transfers between devices with their start and end apart: 10 -> 16, of which waited for: 6 -> 6; matrix products, arithmetic and copies ran while one was open for 15% -> 18% of each run, Pallas kernels for 15% -> 15%
where the time goes in v1:
time: 571 us; the launch traced here: 563 us
  waiting for transfers between devices  269 us (47%)
  Pallas kernels  115 us (20%)
  other arithmetic  89.8 us (16%)
  starting transfers between devices  43 us (8%)
  local copies, waits for them, and re-layouts  25.8 us (5%)
  between operations  17.5 us (3%)
    psum x1, waiting for transfers between devices, chain(): raw_cols = lax.psum(jnp.where(row_now == slice_root, picked, 0.0), 'row')  163 us
    psum x1, waiting for transfers between devices, chain(): inverse = lax.psum(jnp.where(row_now == 0, inverse, 0.0), 'row')  51.4 us
    pallas_call x1, Pallas kernels, finish(): pl.pallas_call(functools.partial(final_kernel, cols_blocks, runs), grid=(...  49.6 us
    psum x1, waiting for transfers between devices, body(): panel_tiles = lax.psum(panel_tiles, 'col')  31.2 us
    another operation x6, other arithmetic, lower_of(): return jnp.linalg.cholesky(jnp.tril(block) + jnp.tril(block, -1).T)  24.8 us
    another operation x5, other arithmetic, inverse_of(): jax.scipy.linalg.solve_triangular(block, jnp.eye(NB, dtype=jnp.float32),...  20.9 us
    pallas_call x1, Pallas kernels, spread(): pl.pallas_call(functools.partial(spread_kernel, width, stride), out_shape...  20.8 us
    all_to_all x1, waiting for transfers between devices, body(): arrived = lax.all_to_all(outgoing, ('row', 'col'), 0, 0, tiled=True)  13.3 us
  transfers between devices with their start and end apart: 16, of which 6 were waited for; matrix products, arithmetic and copies ran while one was open for 18% of the time, Pallas kernels for 15%

profile of v1, /device:TPU:7, one launch (start us, length us, event | category | flops | bytes accessed | tf_op | source)
XLA Modules:
  0.0 562.9 jit_solution(11918280983327775693)
XLA Ops:
  9.4 7.1 %shard_map.48 = f32[20,128,128]{2,1,0:T(8,128)S(1)} custom-call(s32[128]{0:T(128)S(1)} %get-tuple-element.333.slot_ref, s32[128]{0:T(128)} %valid_ref.1, f32[128,128,128]{2,1,0:T(8,128)} %tiles_ref.1), custom_call_target="tpu_custom_call" | custom-call | tf_op jit(solution)/shard_map/pallas_call | solution.py:57
  17.5 3.2 collective-permute-start.5
  21.2 3.8 fusion.130
  32.8 20.8 %shard_map.50 = (f32[32,82,8,128]{3,2,1,0:T(8,128)S(1)}, s32[32,128]{1,0:T(8,128)}) custom-call(s32[6,128]{1,0:T(8,128)S(1)} %select_reduce_fusion.8.meta_ref, s32[2,16]{1,0:T(2,128)S(1)} %select_reduce_fusion.12.empty_ref, s32[3]{0:T(128)S(1)} %pad_add_fusion.2.count_ref, f32[128,16,8,128]{3,2,1,0:T(8,128)} %bitcast.155), custom_call_target="tpu_custom_call" | custom-call | tf_op jit(solution)/shard_map/pallas_call | solution.py:123
  53.7 4.2 copy-done.5
  58.0 3.4 broadcast_select_fusion.3
  69.3 2.3 shard_map.49
  71.7 10.0 %all-to-all-start.2 = ((s32[32,1,82]{2,1,0:T(1,128)}), s32[32,1,82]{2,1,0:T(1,128)S(1)}, u32[]{:S(2)}, u32[]{:S(2)}) async-start(s32[32,1,82]{2,1,0:T(1,128)} %bitcast.35), calls=%async_computation.2 | async-start | bytes 32768 | tf_op jit(solution)/shard_map/all_to_all | solution.py:620
  84.9 9.4 %all-to-all-done.2 = s32[32,1,82]{2,1,0:T(1,128)S(1)} async-done(((s32[32,1,82]{2,1,0:T(1,128)}), s32[32,1,82]{2,1,0:T(1,128)S(1)}, u32[]{:S(2)}, u32[]{:S(2)}) %all-to-all-start.2) | async-done | bytes 10528 | tf_op jit(solution)/shard_map/all_to_all | solution.py:620
  95.6 3.3 broadcast_select_fusion.2
  100.2 3.2 broadcast_select_fusion.5
  104.7 6.1 %convert_reduce_fusion.1 = s32[2624]{0:T(1024)S(1)} fusion(s32[2624]{0:T(1024)S(1)} %get-tuple-element.328, s32[2624]{0:T(1024)S(1)} %get-tuple-element.327), kind=kLoop, calls=%fused_computation.104 | loop fusion | flops 34424256 | bytes 31488 | tf_op jit(solution)/shard_map/reduce_sum | solution.py:633
  116.7 31.2 %all-reduce.17.cloned.1.call-done.arrived_ref = f32[32,128,128]{2,1,0:T(8,128)} async-done(((f32[32,128,128]{2,1,0:T(8,128)}), f32[32,128,128]{2,1,0:T(8,128)}) %all-reduce.17.cloned.1.call-update) | async-done | bytes 2097168 | tf_op jit(solution)/shard_map/psum | solution.py:619
  147.9 6.2 %all-to-all-start.3 = ((s32[32,1,53]{2,1,0:T(1,128)}), s32[32,1,53]{2,1,0:T(1,128)S(1)}, u32[]{:S(2)}, u32[]{:S(2)}) async-start(s32[32,1,53]{2,1,0:T(1,128)} %bitcast.41), calls=%async_computation.3 | async-start | bytes 32768 | tf_op jit(solution)/shard_map/all_to_all | solution.py:648
  154.1 5.3 maximum_select_fusion.front_ref
  159.5 5.9 %all-to-all-start.4 = ((f32[32,82,8,128]{3,2,1,0:T(8,128)}), f32[32,82,8,128]{3,2,1,0:T(8,128)}, u32[]{:S(2)}, u32[]{:S(2)}) async-start(f32[32,82,8,128]{3,2,1,0:T(8,128)} %copy-done.5), calls=%async_computation.4 | async-start | bytes 21495808 | tf_op jit(solution)/shard_map/all_to_all | solution.py:672
  178.8 11.7 %cholesky.96 = f32[128,128]{1,0:T(8,128)S(1)} custom-call(f32[128,128]{1,0:T(8,128)S(1)} %copy.160), custom_call_target="Cholesky" | custom-call | tf_op jit(solution)/shard_map/jit(cholesky)/cholesky | solution.py:458
  191.9 9.8 %custom-call.10 = f32[1,128,128]{1,2,0:T(8,128)S(1)} custom-call(f32[1,128,128]{2,1,0:T(8,128)S(1)} %get-tuple-element.292), custom_call_target="InvertDiagBlocksLowerTriangular" | custom-call | tf_op jit(solution)/shard_map/jit(_solve_triangular)/triangular_solve | solution.py:461
  201.7 3.1 dynamic-slice_select_fusion.1
  206.1 11.7 %cholesky.107 = f32[128,128]{1,0:T(8,128)S(1)} custom-call(f32[128,128]{1,0:T(8,128)S(1)} %fusion.47), custom_call_target="Cholesky" | custom-call | tf_op jit(solution)/shard_map/jit(cholesky)/cholesky | solution.py:458
  219.2 9.8 %custom-call.11 = f32[1,128,128]{1,2,0:T(8,128)S(1)} custom-call(f32[1,128,128]{2,1,0:T(8,128)S(1)} %get-tuple-element.290), custom_call_target="InvertDiagBlocksLowerTriangular" | custom-call | tf_op jit(solution)/shard_map/jit(_solve_triangular)/triangular_solve | solution.py:461
  230.0 162.7 %all-reduce.19.cloned.1.call-done.raw_ref = f32[2048,256]{1,0:T(8,128)} async-done(((f32[2048,256]{1,0:T(8,128)}), f32[2048,256]{1,0:T(8,128)}) %all-reduce.19.cloned.1.call-update) | async-done | bytes 2097168 | tf_op jit(solution)/shard_map/psum | solution.py:678
  396.3 51.4 %all-reduce.21.cloned.1.call-done.inverse_ref = f32[256,256]{1,0:T(8,128)} async-done(((f32[256,256]{1,0:T(8,128)}), f32[256,256]{1,0:T(8,128)}) %all-reduce.21.cloned.1.call-update) | async-done | bytes 262160 | tf_op jit(solution)/shard_map/psum | solution.py:682
  447.7 2.2 copy-done.2
  450.8 7.5 %shard_map.52 = (f32[4096,256]{1,0:T(8,128)}, bf16[4096,768]{1,0:T(8,128)(2,1)}) custom-call(f32[4096,256]{1,0:T(8,128)S(1)} %copy-done.2, f32[256,256]{1,0:T(8,128)S(1)} %copy-done.14), custom_call_target="tpu_custom_call" | custom-call | tf_op jit(solution)/shard_map/pallas_call | solution.py:331
  458.3 4.3 shard_map.53
  462.6 13.3 %all-to-all-done.4 = f32[32,82,8,128]{3,2,1,0:T(8,128)} async-done(((f32[32,82,8,128]{3,2,1,0:T(8,128)}), f32[32,82,8,128]{3,2,1,0:T(8,128)}, u32[]{:S(2)}, u32[]{:S(2)}) %all-to-all-start.4) | async-done | bytes 10747936 | tf_op jit(solution)/shard_map/all_to_all | solution.py:672
  475.9 79.9 %conditional.1 = (f32[4096,2048]{1,0:T(8,128)}) conditional(s32[]{:T(128)} %convert_element_type.74, (s32[32,82]{1,0:T(8,128)}, s32[32,82]{0,1:T(8,128)S(1)}, s32[2]{0:T(128)}, f32[4096,2048]{1,0:T(8,128)}, f32[4096,256]{1,0:T(8,128)}, /*index=5*/bf16[4096,768]{1,0:T(8,128)(2,1)}, f32[256,2048]{1,0:T(8,128)}, bf16[768,2048]{1,0:T(8,128)(2,1)}, ...), branch_computations={%region_29.33_spmd, %region_30.40_spmd} | conditional | flops 158879152 | bytes 287434368 | solution.py:721
  475.9 9.4 %branch_0_fun.4 = f32[832,8,128]{2,1,0:T(8,128)} custom-call(s32[32,82]{1,0:T(8,128)S(1)} %get-tuple-element.110.slot_ref, f32[32,82,8,128]{3,2,1,0:T(8,128)} %get-tuple-element.109.arrived_ref), custom_call_target="tpu_custom_call" | custom-call | tf_op jit(solution)/shard_map/cond/branch_0_fun/pallas_call | solution.py:156
  485.3 5.9 %all-to-all-start = ((f32[16,52,8,128]{3,2,1,0:T(8,128)}), f32[16,52,8,128]{3,2,1,0:T(8,128)S(1)}, u32[]{:S(2)}, u32[]{:S(2)}) async-start(f32[16,52,8,128]{3,2,1,0:T(8,128)} %bitcast), calls=%async_computation | async-start | bytes 6815744 | tf_op jit(solution)/shard_map/cond/branch_0_fun/all_to_all | solution.py:693
  491.9 49.6 %branch_0_fun.3.partial_ref = f32[4096,2048]{1,0:T(8,128)} custom-call(s32[32,82]{1,0:T(8,128)S(1)} %copy-done.20, s32[32,82]{1,0:T(8,128)} %copy.169.run_ref, s32[2]{0:T(128)S(1)} %copy-done.26, f32[4096,2048]{1,0:T(8,128)} %get-tuple-element.103.front_ref, f32[4096,256]{1,0:T(8,128)} %get-tuple-element.104.rows_ref, ...), custom_call_target="tpu_custom_call" | custom-call | tf_op jit(solution)/shard_map/cond/branch_0_fun/pallas_call | solution.py:441
  542.9 11.8 %branch_0_fun.5 = f32[4096,2048]{1,0:T(8,128)} custom-call(s32[832]{0:T(1024)S(1)} %copy-done.23, s32[832]{0:T(1024)S(1)} %copy-done.22, s32[832]{0:T(1024)S(1)} %copy-done.21, s32[1]{0:T(128)} %get-tuple-element.99.count_ref, f32[4096,2048]{1,0:T(8,128)} %branch_0_fun.3.partial_ref, f32[832,8,128]{2,1,0:T(8,128)S(1)} %bitcast.154), custom_call_target="tpu_custom_call", output_to_operand_aliasing={{}: (4, {})} | custom-call | tf_op jit(solution)/shard_map/cond/branch_0_fun/pallas_call | solution.py:235
  (178 shorter events, 54.7 us)
Async XLA Ops:
  7.4 23.9 %copy-start.19 = (s32[32,128]{1,0:T(8,128)}, s32[32,128]{1,0:T(8,128)S(1)}, u32[]{:S(2)}) copy-start(s32[32,128]{1,0:T(8,128)S(1)} %get-tuple-element.316) | copy-start | bytes 49156
  17.5 50.7 %collective-permute-start.5 = (f32[5,128,128]{2,1,0:T(8,128)}, f32[5,128,128]{2,1,0:T(8,128)S(1)}, u32[]{:S(2)}, u32[]{:S(2)}) collective-permute-start(f32[5,128,128]{2,1,0:T(8,128)} %get-tuple-element.311), channel_id=1, source_target_pairs={{0,24},{8,0},{16,8},{24,16},{1,25},{9,1},{17,9},{25,17},{2,26},{10... | collective-permute-start | bytes 983048 | tf_op jit(solution)/shard_map/ppermute | solution.py:539
  20.7 47.4 %collective-permute-start.4 = (f32[5,128,128]{2,1,0:T(8,128)}, f32[5,128,128]{2,1,0:T(8,128)}, u32[]{:S(2)}, u32[]{:S(2)}) collective-permute-start(f32[5,128,128]{2,1,0:T(8,128)} %get-tuple-element.312), channel_id=1, source_target_pairs={{0,16},{8,24},{16,0},{24,8},{1,17},{9,25},{17,1},{25,9},{2,18},{10... | collective-permute-start | bytes 983048 | tf_op jit(solution)/shard_map/ppermute | solution.py:539
  20.7 8.3 %copy-start.24 = (s32[128]{0:T(128)S(1)}, s32[128]{0:T(128)}, u32[]{:S(2)}) copy-start(s32[128]{0:T(128)} %valid_ref.1) | copy-start | bytes 1540
  20.7 47.4 %collective-permute-start.3 = (f32[5,128,128]{2,1,0:T(8,128)S(1)}, f32[5,128,128]{2,1,0:T(8,128)}, u32[]{:S(2)}, u32[]{:S(2)}) collective-permute-start(f32[5,128,128]{2,1,0:T(8,128)S(1)} %get-tuple-element.313), channel_id=1, source_target_pairs={{0,8},{8,16},{16,24},{24,0},{1,9},{9,17},{17,25},{25,1},{2,10},{10... | collective-permute-start | bytes 983048 | tf_op jit(solution)/shard_map/ppermute | solution.py:539
  25.0 28.7 %copy-start.16 = (f32[2048,256]{1,0:T(8,128)}, f32[2048,256]{1,0:T(8,128)S(1)}, u32[]{:S(2)}) copy-start(f32[2048,256]{1,0:T(8,128)S(1)} %get-tuple-element.172) | copy-start | bytes 6291460
  25.0 33.0 %collective-permute-start.7 = (f32[2048,256]{1,0:T(8,128)}, f32[2048,256]{1,0:T(8,128)}, u32[]{:S(2)}, u32[]{:S(2)}) collective-permute-start(f32[2048,256]{1,0:T(8,128)} %get-tuple-element.174), channel_id=1, source_target_pairs={{0,4},{8,12},{16,20},{24,28}} | collective-permute-start | bytes 6291464 | tf_op jit(solution)/shard_map/ppermute | solution.py:477
  27.0 30.9 %collective-permute-start.6 = (f32[2048,256]{1,0:T(8,128)S(1)}, f32[2048,256]{1,0:T(8,128)}, u32[]{:S(2)}, u32[]{:S(2)}) collective-permute-start(f32[2048,256]{1,0:T(8,128)S(1)} %get-tuple-element.172), channel_id=1, source_target_pairs={{0,2},{8,10},{16,18},{24,26}} | collective-permute-start | bytes 6291464 | tf_op jit(solution)/shard_map/ppermute | solution.py:476
  53.7 4.2 copy-start.5
  58.0 5.5 copy-start.17
  61.3 6.0 %copy-start.18 = (s32[2,4096]{1,0:T(2,128)S(1)}, s32[2,4096]{1,0:T(2,128)}, u32[]{:S(2)}) copy-start(s32[2,4096]{1,0:T(2,128)} %param.15) | copy-start | bytes 98308
  61.3 34.3 %collective-permute-start.9 = (f32[2048,256]{1,0:T(8,128)}, f32[2048,256]{1,0:T(8,128)}, u32[]{:S(2)}, u32[]{:S(2)}) collective-permute-start(f32[2048,256]{1,0:T(8,128)} %broadcast_select_fusion.3), channel_id=1, source_target_pairs={{0,2},{4,6},{8,10},{12,14},{16,18},{20,22},{24,26},{28,30}} | collective-permute-start | bytes 6291464 | tf_op jit(solution)/shard_map/ppermute | solution.py:485
  65.3 34.9 %collective-permute-start.8 = (f32[2048,256]{1,0:T(8,128)S(1)}, f32[2048,256]{1,0:T(8,128)}, u32[]{:S(2)}, u32[]{:S(2)}) collective-permute-start(f32[2048,256]{1,0:T(8,128)S(1)} %broadcast_select_fusion.4), channel_id=1, source_target_pairs={{0,4},{2,6},{8,12},{10,14},{16,20},{18,22},{24,28},{26,30}} | collective-permute-start | bytes 6291464 | tf_op jit(solution)/shard_map/ppermute | solution.py:484
  71.7 22.6 %all-to-all-start.2 = ((s32[32,1,82]{2,1,0:T(1,128)}), s32[32,1,82]{2,1,0:T(1,128)S(1)}, u32[]{:S(2)}, u32[]{:S(2)}) async-start(s32[32,1,82]{2,1,0:T(1,128)} %bitcast.35), calls=%async_computation.2 | async-start | bytes 32768 | tf_op jit(solution)/shard_map/all_to_all | solution.py:620
  81.7 66.2 %all-reduce.17.cloned.1.call-start = ((), (), s32[]{:S(2)}) async-start(), calls=%async_computation.8 | async-start | bytes 4194304 | tf_op jit(solution)/shard_map/psum | solution.py:619
  98.9 55.2 %collective-permute-start.11 = (f32[2048,256]{1,0:T(8,128)}, f32[2048,256]{1,0:T(8,128)}, u32[]{:S(2)}, u32[]{:S(2)}) collective-permute-start(f32[2048,256]{1,0:T(8,128)} %broadcast_select_fusion.2), channel_id=1, source_target_pairs={{0,1},{2,3},{4,5},{6,7},{8,9},{10,11},{12,13},{14,15},{16,17},{18,... | collective-permute-start | bytes 6291464 | tf_op jit(solution)/shard_map/ppermute | solution.py:489
  103.3 50.8 %collective-permute-start.10 = (f32[2048,256]{1,0:T(8,128)}, f32[2048,256]{1,0:T(8,128)S(1)}, u32[]{:S(2)}, u32[]{:S(2)}) collective-permute-start(f32[2048,256]{1,0:T(8,128)} %broadcast_select_fusion.5), channel_id=1, source_target_pairs={{0,1},{2,3},{4,5},{6,7},{8,9},{10,11},{12,13},{14,15},{16,17},{18,... | collective-permute-start | bytes 6291464 | tf_op jit(solution)/shard_map/ppermute | solution.py:488
  147.9 11.6 %all-to-all-start.3 = ((s32[32,1,53]{2,1,0:T(1,128)}), s32[32,1,53]{2,1,0:T(1,128)S(1)}, u32[]{:S(2)}, u32[]{:S(2)}) async-start(s32[32,1,53]{2,1,0:T(1,128)} %bitcast.41), calls=%async_computation.3 | async-start | bytes 32768 | tf_op jit(solution)/shard_map/all_to_all | solution.py:648
  159.5 316.5 %all-to-all-start.4 = ((f32[32,82,8,128]{3,2,1,0:T(8,128)}), f32[32,82,8,128]{3,2,1,0:T(8,128)}, u32[]{:S(2)}, u32[]{:S(2)}) async-start(f32[32,82,8,128]{3,2,1,0:T(8,128)} %copy-done.5), calls=%async_computation.4 | async-start | bytes 21495808 | tf_op jit(solution)/shard_map/all_to_all | solution.py:672
  165.4 7.2 %copy-start.12 = (f32[32,128,128]{2,1,0:T(8,128)S(1)}, f32[32,128,128]{2,1,0:T(8,128)}, u32[]{:S(2)}) copy-start(f32[32,128,128]{2,1,0:T(8,128)} %all-reduce.17.cloned.1.call-done.arrived_ref) | copy-start | bytes 6291460
  165.4 227.3 %all-reduce.19.cloned.1.call-start = ((), (), s32[]{:S(2)}) async-start(), calls=%async_computation.9 | async-start | bytes 4194304 | tf_op jit(solution)/shard_map/psum | solution.py:678
  172.6 2.2 copy-start.3
  176.5 1.9 copy-start.1
  204.7 242.9 %all-reduce.21.cloned.1.call-start = ((), (), s32[]{:S(2)}) async-start(), calls=%async_computation.10 | async-start | bytes 524288 | tf_op jit(solution)/shard_map/psum | solution.py:682
  447.7 2.2 copy-start.2
  450.8 7.5 %copy-start.10 = (f32[2048,256]{1,0:T(8,128)S(1)}, f32[2048,256]{1,0:T(8,128)}, u32[]{:S(2)}) copy-start(f32[2048,256]{1,0:T(8,128)} %all-reduce.19.cloned.1.call-done.raw_ref) | copy-start | bytes 6291460
  485.3 6.6 %copy-start.20 = (s32[32,82]{1,0:T(8,128)S(1)}, s32[32,82]{1,0:T(8,128)}, u32[]{:S(2)}) copy-start(s32[32,82]{1,0:T(8,128)} %get-tuple-element.100.code_ref) | copy-start | bytes 31492 | tf_op jit(solution)/shard_map/cond
  485.3 6.6 %copy-start.26 = (s32[2]{0:T(128)S(1)}, s32[2]{0:T(128)}, u32[]{:S(2)}) copy-start(s32[2]{0:T(128)} %get-tuple-element.102.place_ref) | copy-start | bytes 28 | tf_op jit(solution)/shard_map/cond
  485.3 57.6 %all-to-all-start = ((f32[16,52,8,128]{3,2,1,0:T(8,128)}), f32[16,52,8,128]{3,2,1,0:T(8,128)S(1)}, u32[]{:S(2)}, u32[]{:S(2)}) async-start(f32[16,52,8,128]{3,2,1,0:T(8,128)} %bitcast), calls=%async_computation | async-start | bytes 6815744 | tf_op jit(solution)/shard_map/cond/branch_0_fun/all_to_all | solution.py:693
  491.9 51.0 %copy-start.21 = (s32[832]{0:T(1024)S(1)}, s32[832]{0:T(1024)}, u32[]{:S(2)}) copy-start(s32[832]{0:T(1024)} %get-tuple-element.98.index_ref) | copy-start | bytes 9988 | tf_op jit(solution)/shard_map/cond
  491.9 51.0 %copy-start.22 = (s32[832]{0:T(1024)S(1)}, s32[832]{0:T(1024)}, u32[]{:S(2)}) copy-start(s32[832]{0:T(1024)} %get-tuple-element.97.unit_ref) | copy-start | bytes 9988 | tf_op jit(solution)/shard_map/cond
  491.9 51.0 %copy-start.23 = (s32[832]{0:T(1024)S(1)}, s32[832]{0:T(1024)}, u32[]{:S(2)}) copy-start(s32[832]{0:T(1024)} %get-tuple-element.96.block_ref) | copy-start | bytes 9988 | tf_op jit(solution)/shard_map/cond
  (1 other events, 0.9 us)
Sparse Core Ops, SparseCore 0:
  86.1 61.7 all-reduce.16
  204.9 187.7 all-reduce.18
  395.0 52.5 all-reduce.20
